TPU v7x, 512 devices: a whole 4x4x16 slice. The times are simulated.
512 devices in a mesh: cube: 8 (over x, core), front: 64 (over z, y).
Axes of the slice: x: 4, y: 4, z: 16, core: 2. Of those that a mesh axis runs over, the one named last changes fastest.
Arguments:
- leaf_blocks: float32 [8, 3840, 3840], P('cube', 'front'), may hold values from -8 to 11, as said below
- front_entries: float32 [7, 4096, 256], P(None, 'front'), may hold values from -0.001 to 3
- child_maps: int32 [7, 2, 60], replicated, may hold values from 0 to 63, as said below
Outputs:
- factor_columns: float32 [8, 3, 4096, 256], P('cube', None, 'front')
- top_block: float32 [3840, 3840], P('front')
Inputs may be any that keep to these rules, and one draw needn't show every extreme that they name: `child_maps`: for each node, each of the two rows lists distinct offsets, and the two rows together name every offset from 0 to 63. `leaf_blocks`: each leaf block is symmetric positive definite.
All inputs are finite; a program needn't handle non-finite values.
Results may differ from a plain program's by a relative error of at most 0.00033.
Values may be sent and summed in bfloat16 or wider, within the bound.
No kernel may reach another device: no remote copies, remote signals or barrier semaphores. Data moves between devices by JAX's collectives and lax.ppermute only.
A program may use at most 128 MiB of HBM per device.

v0:
```python
import jax
import jax.numpy as jnp
from jax import lax
from jax.sharding import PartitionSpec as P

PANEL = 256
HIGH = lax.Precision.HIGHEST


def swapped(value, axis, apart):
    mask = 2**apart
    pairs = [(source, source ^ mask) for source in range(lax.axis_size(axis))]
    return lax.ppermute(value, axis, pairs)


def onehot_table(mapping, width):
    return (mapping[:, None] == jnp.arange(width, dtype=jnp.int32)[None, :]).astype(jnp.float32)


def scatter_rows(block, mapping, devices, width):
    block_rows = block.shape[0]
    table = onehot_table(mapping, width)
    grid = block.reshape(block_rows, devices, block_rows)
    widened = jnp.einsum("ubv,vs->usb", grid, table, precision=HIGH)
    placed = jnp.einsum("usb,ut->tsb", widened, table, precision=HIGH)
    return placed.reshape(width, width * devices)


def cholesky_lower(pivot):
    symmetric = jnp.tril(pivot) + jnp.tril(pivot, -1).T
    return jnp.linalg.cholesky(symmetric)


def factor_front(matrix, devices, position, width, panel_rows):
    panel = panel_rows * devices
    trailing = width - panel_rows
    last_col = panel_rows * devices
    local_pivot = matrix[0:panel_rows, 0:last_col]
    gathered = lax.all_gather(local_pivot, "front", axis=0, tiled=True)
    pivot = jnp.transpose(gathered.reshape(devices, panel_rows, panel), (1, 0, 2)).reshape(
        panel, panel
    )
    factor = cholesky_lower(pivot)
    lhs_rows = matrix[panel_rows:, 0:last_col]
    solved = jax.scipy.linalg.solve_triangular(factor, lhs_rows.T, lower=True).T
    rounded = solved.astype(jnp.bfloat16)
    update = jnp.einsum(
        "ip,jp->ij",
        rounded,
        lax.all_gather(rounded, "front", axis=0, tiled=True),
        preferred_element_type=jnp.float32,
    )
    reordered = jnp.transpose(update.reshape(trailing, devices, trailing), (0, 2, 1)).reshape(
        trailing, trailing * devices
    )
    matrix = matrix.at[panel_rows:, last_col:].add(-reordered)
    upper = jnp.zeros((0, panel), jnp.float32)
    middle = lax.dynamic_index_in_dim(
        factor.reshape(panel_rows, devices, panel), position, 1, keepdims=False
    )
    columns = jnp.concatenate([upper, middle, solved], axis=0)
    return (columns, matrix)


def on_device(leaf_blocks, front_entries, child_maps):
    devices = lax.axis_size("front")
    position = lax.axis_index("front")
    subcube = lax.axis_index("cube")
    cube_count = lax.axis_size("cube")
    heights = cube_count.bit_length() - 1
    width = front_entries.shape[1]
    sep_rows = front_entries.shape[2] // devices
    panel_rows = PANEL // devices
    block_rows = leaf_blocks.shape[1]
    current = leaf_blocks[0]
    factors = []
    for height in range(heights):
        sibling = swapped(current, "cube", height)
        side_bit = jnp.right_shift(subcube, height) & 1
        left_block = jnp.where(side_bit == 0, current, sibling)
        right_block = jnp.where(side_bit == 0, sibling, current)
        node = jnp.right_shift(subcube + cube_count, height + 1)
        entries = lax.dynamic_index_in_dim(front_entries, node - 1, 0, keepdims=False)
        mappings = lax.dynamic_index_in_dim(child_maps, node - 1, 0, keepdims=False)
        placed_entries = jnp.transpose(
            entries.reshape(width, devices, sep_rows), (0, 2, 1)
        ).reshape(width, sep_rows * devices)
        zeros_rest = jnp.zeros((width, (width - sep_rows) * devices), jnp.float32)
        matrix = jnp.concatenate([placed_entries, zeros_rest], axis=1)
        matrix = matrix + scatter_rows(left_block, mappings[0], devices, width)
        matrix = matrix + scatter_rows(right_block, mappings[1], devices, width)
        factor_part, matrix = factor_front(matrix, devices, position, width, panel_rows)
        factors.append(factor_part)
        remain = matrix[sep_rows:, sep_rows * devices :].reshape(block_rows, block_rows, devices)
        current = jnp.transpose(remain, (0, 2, 1)).reshape(block_rows, devices * block_rows)
    return (jnp.stack(factors)[None], current)


def solution(mesh):
    in_specs = (P("cube", "front", None), P(None, "front", None), P())
    out_specs = (P("cube", None, "front", None), P("front", None))
    return jax.shard_map(
        on_device, mesh=mesh, in_specs=in_specs, out_specs=out_specs, check_vma=False
    )
```

profile of v0, /device:TPU:2, one launch (start us, length us, event | category | flops | bytes accessed | tf_op | source)
XLA Modules:
  0.0 1041.9 jit_solution(18427782496393358375)
XLA Ops:
  8.5 1.9 collective-permute-start
  14.8 4.3 reshape.238
  19.1 2.9 convolution_bitcast_fusion.5
  22.0 2.4 fusion.10
  27.4 2.9 reshape.240
  30.3 2.9 convolution_bitcast_fusion.4
  33.2 2.9 fusion.8
  40.7 88.9 %all-gather = f32[64,4,256]{2,1,0:T(4,128)S(1)} all-gather(f32[1,4,256]{2,1,0:T(4,128)S(1)} %slice_bitcast_fusion.17), channel_id=1, replica_groups=mesh['cube'=8,'front'=64] {'front'}, dimensions={0}, use_global_device_ids=true | all-gather | bytes 266240 | tf_op jit(solution)/shard_map/all_gather | solution.py:39
  130.1 11.7 %cholesky.172 = f32[128,128]{1,0:T(8,128)S(1)} custom-call(f32[128,128]{1,0:T(8,128)S(1)} %copy.109), custom_call_target="Cholesky" | custom-call | tf_op jit(solution)/shard_map/jit(cholesky)/cholesky | solution.py:31
  141.9 9.8 custom-call.15
  152.4 11.7 %cholesky.189 = f32[128,128]{1,0:T(8,128)S(1)} custom-call(f32[128,128]{1,0:T(8,128)S(1)} %copy.111), custom_call_target="Cholesky" | custom-call | tf_op jit(solution)/shard_map/jit(cholesky)/cholesky | solution.py:31
  166.1 4.0 while.9
  170.1 19.7 %custom-call.16 = f32[2,128,128]{1,2,0:T(8,128)S(1)} custom-call(f32[2,128,128]{2,1,0:T(8,128)S(1)} %get-tuple-element.60), custom_call_target="InvertDiagBlocksLowerTriangular" | custom-call | tf_op jit(solution)/shard_map/jit(_solve_triangular)/triangular_solve | solution.py:45
  191.1 136.6 %all-gather.10.cloned.1.call-done = bf16[64,60,256]{2,1,0:T(8,128)(2,1)} async-done(((bf16[1,60,256]{2,1,0:T(8,128)(2,1)}), bf16[64,60,256]{2,1,0:T(8,128)(2,1)}) %all-gather.10.cloned.1.call-update) | async-done | bytes 1966096 | tf_op jit(solution)/shard_map/all_gather | solution.py:50
  327.7 2.5 reshape.297
  331.9 4.1 neg.37
  335.9 1.9 copy.114
  337.9 2.1 neg.39
  341.0 2.0 reshape.247
  343.0 1.9 copy.115
  344.9 2.8 reshape.248
  347.8 2.5 collective-permute-start.1
  350.6 13.7 %collective-permute-done.1 = f32[60,3840]{1,0:T(8,128)S(1)} collective-permute-done((f32[60,3840]{1,0:T(8,128)S(1)}, f32[60,3840]{1,0:T(8,128)S(1)}, u32[]{:S(2)}, u32[]{:S(2)}) %collective-permute-start.1) | collective-permute-done | bytes 921632 | tf_op jit(solution)/shard_map/ppermute | solution.py:13
  365.3 4.5 reshape.249
  369.8 2.9 convolution_bitcast_fusion.3
  372.7 2.4 fusion.6
  378.1 2.9 reshape.251
  381.0 2.9 convolution_bitcast_fusion.2
  383.9 2.6 fusion.4
  391.1 80.7 %all-gather.2 = f32[64,4,256]{2,1,0:T(4,128)S(1)} all-gather(f32[1,4,256]{2,1,0:T(4,128)S(1)} %slice_bitcast_fusion.16), channel_id=1, replica_groups=mesh['cube'=8,'front'=64] {'front'}, dimensions={0}, use_global_device_ids=true | all-gather | bytes 266240 | tf_op jit(solution)/shard_map/all_gather | solution.py:39
  472.3 11.7 %cholesky.206 = f32[128,128]{1,0:T(8,128)S(1)} custom-call(f32[128,128]{1,0:T(8,128)S(1)} %copy.124), custom_call_target="Cholesky" | custom-call | tf_op jit(solution)/shard_map/jit(cholesky)/cholesky | solution.py:31
  484.7 9.8 custom-call.17
  495.2 11.7 %cholesky.223 = f32[128,128]{1,0:T(8,128)S(1)} custom-call(f32[128,128]{1,0:T(8,128)S(1)} %copy.126), custom_call_target="Cholesky" | custom-call | tf_op jit(solution)/shard_map/jit(cholesky)/cholesky | solution.py:31
  509.6 4.2 while.10
  513.8 19.7 %custom-call.18 = f32[2,128,128]{1,2,0:T(8,128)S(1)} custom-call(f32[2,128,128]{2,1,0:T(8,128)S(1)} %get-tuple-element.61), custom_call_target="InvertDiagBlocksLowerTriangular" | custom-call | tf_op jit(solution)/shard_map/jit(_solve_triangular)/triangular_solve | solution.py:45
  534.8 135.8 %all-gather.12.cloned.1.call-done = bf16[64,60,256]{2,1,0:T(8,128)(2,1)} async-done(((bf16[1,60,256]{2,1,0:T(8,128)(2,1)}), bf16[64,60,256]{2,1,0:T(8,128)(2,1)}) %all-gather.12.cloned.1.call-update) | async-done | bytes 1966096 | tf_op jit(solution)/shard_map/all_gather | solution.py:50
  670.7 2.5 reshape.301
  674.8 4.1 neg.41
  678.9 1.9 copy.129
  680.8 2.1 neg.43
  684.0 2.0 reshape.258
  686.0 1.9 copy.130
  687.9 2.9 reshape.259
  690.7 4.0 collective-permute-start.2
  695.9 12.8 %collective-permute-done.2 = f32[60,3840]{1,0:T(8,128)S(1)} collective-permute-done((f32[60,3840]{1,0:T(8,128)S(1)}, f32[60,3840]{1,0:T(8,128)S(1)}, u32[]{:S(2)}, u32[]{:S(2)}) %collective-permute-start.2) | collective-permute-done | bytes 921632 | tf_op jit(solution)/shard_map/ppermute | solution.py:13
  709.8 4.2 reshape.260
  714.1 2.9 convolution_bitcast_fusion.1
  717.0 2.4 fusion.2
  722.3 2.9 reshape.262
  725.2 2.9 convolution_bitcast_fusion
  728.2 2.6 fusion
  735.4 80.7 %all-gather.4 = f32[64,4,256]{2,1,0:T(4,128)S(1)} all-gather(f32[1,4,256]{2,1,0:T(4,128)S(1)} %slice_bitcast_fusion.15), channel_id=1, replica_groups=mesh['cube'=8,'front'=64] {'front'}, dimensions={0}, use_global_device_ids=true | all-gather | bytes 266240 | tf_op jit(solution)/shard_map/all_gather | solution.py:39
  816.6 11.7 %cholesky.240 = f32[128,128]{1,0:T(8,128)S(1)} custom-call(f32[128,128]{1,0:T(8,128)S(1)} %cholesky.276), custom_call_target="Cholesky" | custom-call | tf_op jit(solution)/shard_map/jit(cholesky)/cholesky | solution.py:31
  829.0 9.8 custom-call.19
  839.3 11.7 %cholesky.257 = f32[128,128]{1,0:T(8,128)S(1)} custom-call(f32[128,128]{1,0:T(8,128)S(1)} %convolution_subtract_fusion), custom_call_target="Cholesky" | custom-call | tf_op jit(solution)/shard_map/jit(cholesky)/cholesky | solution.py:31
  853.1 4.3 while.11
  857.3 19.7 %custom-call.20 = f32[2,128,128]{1,2,0:T(8,128)S(1)} custom-call(f32[2,128,128]{2,1,0:T(8,128)S(1)} %get-tuple-element.62), custom_call_target="InvertDiagBlocksLowerTriangular" | custom-call | tf_op jit(solution)/shard_map/jit(_solve_triangular)/triangular_solve | solution.py:45
  879.9 134.3 %all-gather.14.cloned.1.call-done = bf16[64,60,256]{2,1,0:T(8,128)(2,1)} async-done(((bf16[1,60,256]{2,1,0:T(8,128)(2,1)}), bf16[64,60,256]{2,1,0:T(8,128)(2,1)}) %all-gather.14.cloned.1.call-update) | async-done | bytes 1966096 | tf_op jit(solution)/shard_map/all_gather | solution.py:50
  1014.2 2.5 reshape.305
  1018.3 4.1 neg.45
  1022.4 1.9 copy.139
  1024.3 2.1 neg.47
  1027.5 2.0 reshape.267
  1031.4 3.5 reshape.268
  (158 shorter events, 66.0 us)
Async XLA Ops:
  7.2 6.5 copy-start
  7.2 320.5 %all-gather.10.cloned.1.call-start = ((), (), s32[]{:S(2)}) async-start(), calls=%async_computation | async-start | bytes 2129920 | tf_op jit(solution)/shard_map/all_gather | solution.py:50
  8.5 5.2 collective-permute-start
  129.8 36.2 %copy-start.3 = (s32[2]{0:T(128)S(1)}, s32[2]{0:T(128)}, u32[]{:S(2)}) copy-start(s32[2]{0:T(128)} %iota_multiply_fusion) | copy-start | bytes 28
  191.1 479.6 %all-gather.12.cloned.1.call-start = ((), (), s32[]{:S(2)}) async-start(), calls=%async_computation.1 | async-start | bytes 2129920 | tf_op jit(solution)/shard_map/all_gather | solution.py:50
  347.8 16.5 %collective-permute-start.1 = (f32[60,3840]{1,0:T(8,128)S(1)}, f32[60,3840]{1,0:T(8,128)S(1)}, u32[]{:S(2)}, u32[]{:S(2)}) collective-permute-start(f32[60,3840]{1,0:T(8,128)S(1)} %reshape.248), channel_id=1, source_target_pairs={{0,128},{64,192},{128,0},{192,64},{256,384},{320,448},{384,256},{4... | collective-permute-start | bytes 2764808 | tf_op jit(solution)/shard_map/ppermute | solution.py:13
  534.8 479.4 %all-gather.14.cloned.1.call-start = ((), (), s32[]{:S(2)}) async-start(), calls=%async_computation.2 | async-start | bytes 2129920 | tf_op jit(solution)/shard_map/all_gather | solution.py:50
  687.9 7.7 copy-start.1
  690.7 18.0 %collective-permute-start.2 = (f32[60,3840]{1,0:T(8,128)S(1)}, f32[60,3840]{1,0:T(8,128)S(1)}, u32[]{:S(2)}, u32[]{:S(2)}) collective-permute-start(f32[60,3840]{1,0:T(8,128)S(1)} %reshape.259), channel_id=1, source_target_pairs={{0,256},{64,320},{128,384},{192,448},{256,0},{320,64},{384,128},{4... | collective-permute-start | bytes 2764808 | tf_op jit(solution)/shard_map/ppermute | solution.py:13
  733.7 82.7 %copy-start.2 = (pred[256,256]{1,0:T(8,128)(4,1)S(1)}, pred[256,256]{1,0:T(8,128)(4,1)}, u32[]{:S(2)}) copy-start(pred[256,256]{1,0:T(8,128)(4,1)} %copy.136) | copy-start | bytes 196612
Sparse Core Ops, SparseCore 0:
  191.2 136.4 all-gather.9
  534.9 135.7 all-gather.11
  878.4 135.7 all-gather.13
where the time goes:
time: 1050 us; the launch traced here: 1040 us
  waiting for transfers between devices  433 us (41%)
  blocking collectives  250 us (24%)
  other arithmetic  178 us (17%)
  local copies, waits for them, and re-layouts  111 us (11%)
  matrix products  41.4 us (4%)
  between operations  18.8 us (2%)
    all_gather x3, waiting for transfers between devices, factor_front(): lax.all_gather(rounded, 'front', axis=0, tiled=True)  407 us
    all_gather x3, blocking collectives, factor_front(): gathered = lax.all_gather(local_pivot, 'front', axis=0, tiled=True)  250 us
    another operation x20, other arithmetic, cholesky_lower(): return jnp.linalg.cholesky(symmetric)  103 us
    another operation x7, other arithmetic, factor_front(): solved = jax.scipy.linalg.solve_triangular(factor, lhs_rows.T, lower=True).T  60.4 us
    ppermute x3, waiting for transfers between devices, swapped(): return lax.ppermute(value, axis, pairs)  26.5 us
    neg x9, local copies, waits for them, and re-layouts, factor_front(): matrix = matrix.at[panel_rows:, last_col:].add(-reordered)  24.2 us
    reshape x6, local copies, waits for them, and re-layouts, scatter_rows(): grid = block.reshape(block_rows, devices, block_rows)  21.7 us
  transfers between devices with their start and end apart: 6, of which 5 were waited for; matrix products, arithmetic and copies ran while one was open for 1% of the time, Pallas kernels for 0%

commit v1 on v0

--- a/solution.py
+++ b/solution.py
@@ -5,6 +5,12 @@
 
 PANEL = 256
 HIGH = lax.Precision.HIGHEST
+
+
+def gather_by_exchange(x, axis, dim):
+    length = lax.axis_size(axis)
+    repeats = [length if d == dim else 1 for d in range(x.ndim)]
+    return lax.all_to_all(jnp.tile(x, repeats), axis, split_axis=dim, concat_axis=dim, tiled=True)
 
 
 def swapped(value, axis, apart):
@@ -47,7 +53,7 @@
     update = jnp.einsum(
         "ip,jp->ij",
         rounded,
-        lax.all_gather(rounded, "front", axis=0, tiled=True),
+        gather_by_exchange(rounded, "front", 0),
         preferred_element_type=jnp.float32,
     )
     reordered = jnp.transpose(update.reshape(trailing, devices, trailing), (0, 2, 1)).reshape(

time: 1050 us -> 844 us (0.80)
  the two profiles are of different devices: /device:TPU:2 before, /device:TPU:4 now
where the time goes in v1:
time: 844 us; the launch traced here: 840 us
  blocking collectives  414 us (49%)
  other arithmetic  181 us (21%)
  local copies, waits for them, and re-layouts  90.1 us (11%)
  waiting for transfers between devices  81.1 us (10%)
  matrix products  53.3 us (6%)
  starting transfers between devices  13.1 us (2%)
    all_gather x3, blocking collectives, factor_front(): gathered = lax.all_gather(local_pivot, 'front', axis=0, tiled=True)  254 us
    all_to_all x2, blocking collectives, gather_by_exchange(): lax.all_to_all(jnp.tile(x, repeats), axis, split_axis=dim, concat_axis=di...  161 us
    another operation x20, other arithmetic, cholesky_lower(): return jnp.linalg.cholesky(symmetric)  103 us
    another operation x7, other arithmetic, factor_front(): solved = jax.scipy.linalg.solve_triangular(factor, lhs_rows.T, lower=True).T  61.3 us
    all_to_all x1, waiting for transfers between devices, gather_by_exchange(): lax.all_to_all(jnp.tile(x, repeats), axis, split_axis=dim, concat_axis=di...  53.6 us
    ppermute x3, waiting for transfers between devices, swapped(): return lax.ppermute(value, axis, pairs)  27.5 us
    dot_general x6, matrix products, scatter_rows(): placed = jnp.einsum('usb,ut->tsb', widened, table, precision=HIGH)  24.9 us
    reshape x6, local copies, waits for them, and re-layouts, scatter_rows(): grid = block.reshape(block_rows, devices, block_rows)  21.8 us
  transfers between devices with their start and end apart: 4, of which 4 were waited for; matrix products, arithmetic and copies ran while one was open for 1% of the time, Pallas kernels for 0%

profile of v1, /device:TPU:4, one launch (start us, length us, event | category | flops | bytes accessed | tf_op | source)
XLA Modules:
  0.0 839.9 jit_solution(9639115073263175992)
XLA Ops:
  2.0 1.9 collective-permute-start
  7.5 4.4 reshape.262
  12.0 2.9 convolution_bitcast_fusion.5
  14.9 2.4 fusion.10
  18.6 1.7 reshape.263
  20.3 2.9 reshape.264
  23.2 2.9 convolution_bitcast_fusion.4
  26.1 12.3 %fusion.8 = f32[64,64,64]{2,0,1:T(8,128)S(1)} fusion(f32[60,64,64]{2,1,0:T(8,128)S(1)} %convolution_bitcast_fusion.4, s32[60]{0:T(128)S(1)} %get-tuple-element.128), kind=kOutput, calls=%fused_computation.14 | convolution fusion | flops 188747520 | bytes 2031856 | tf_op jit(solution)/shard_map/usb,ut->tsb/dot_general | solution.py:31
  41.2 1.7 add_add_fusion.2
  42.9 88.9 %all-gather = f32[64,4,256]{2,1,0:T(4,128)S(1)} all-gather(f32[1,4,256]{2,1,0:T(4,128)S(1)} %slice_bitcast_fusion.17), channel_id=1, replica_groups=mesh['cube'=8,'front'=64] {'front'}, dimensions={0}, use_global_device_ids=true | all-gather | bytes 266240 | tf_op jit(solution)/shard_map/all_gather | solution.py:45
  132.4 11.7 %cholesky.172 = f32[128,128]{1,0:T(8,128)S(1)} custom-call(f32[128,128]{1,0:T(8,128)S(1)} %copy.106), custom_call_target="Cholesky" | custom-call | tf_op jit(solution)/shard_map/jit(cholesky)/cholesky | solution.py:37
  144.1 9.8 %custom-call.15 = f32[1,128,128]{1,2,0:T(8,128)S(1)} custom-call(f32[1,128,128]{2,1,0:T(8,128)S(1)} %get-tuple-element.119), custom_call_target="InvertDiagBlocksLowerTriangular" | custom-call | tf_op jit(solution)/shard_map/jit(cholesky)/cholesky | solution.py:37
  154.6 11.7 %cholesky.189 = f32[128,128]{1,0:T(8,128)S(1)} custom-call(f32[128,128]{1,0:T(8,128)S(1)} %copy.108), custom_call_target="Cholesky" | custom-call | tf_op jit(solution)/shard_map/jit(cholesky)/cholesky | solution.py:37
  169.3 4.5 while.9
  173.8 19.7 %custom-call.16 = f32[2,128,128]{1,2,0:T(8,128)S(1)} custom-call(f32[2,128,128]{2,1,0:T(8,128)S(1)} %get-tuple-element.60), custom_call_target="InvertDiagBlocksLowerTriangular" | custom-call | tf_op jit(solution)/shard_map/jit(_solve_triangular)/triangular_solve | solution.py:51
  194.4 91.0 %all_to_all.18 = bf16[64,60,256]{2,1,0:T(8,128)(2,1)S(1)} all-to-all(bf16[64,60,256]{2,1,0:T(8,128)(2,1)S(1)} %tile.6), channel_id=1, replica_groups=mesh['cube'=8,'front'=64] {'front'}, dimensions={0} | all-to-all | bytes 3932160 | tf_op jit(solution)/shard_map/all_to_all | solution.py:13
  285.4 2.4 negate_bitcast_fusion.2
  290.5 2.2 slice_add_fusion.2
  292.8 2.0 reshape.271
  294.8 1.9 copy.113
  296.6 2.8 reshape.272
  299.5 3.1 collective-permute-start.1
  303.0 12.5 %collective-permute-done.1 = f32[60,3840]{1,0:T(8,128)S(1)} collective-permute-done((f32[60,3840]{1,0:T(8,128)S(1)}, f32[60,3840]{1,0:T(8,128)S(1)}, u32[]{:S(2)}, u32[]{:S(2)}) %collective-permute-start.1) | collective-permute-done | bytes 921632 | tf_op jit(solution)/shard_map/ppermute | solution.py:19
  316.9 4.2 reshape.273
  321.2 2.9 convolution_bitcast_fusion.3
  324.1 2.4 fusion.6
  329.4 2.9 reshape.275
  332.3 2.9 convolution_bitcast_fusion.2
  335.3 2.8 fusion.4
  339.3 1.7 reshape.276
  342.7 81.3 %all-gather.1 = f32[64,4,256]{2,1,0:T(4,128)S(1)} all-gather(f32[1,4,256]{2,1,0:T(4,128)S(1)} %slice_bitcast_fusion.16), channel_id=1, replica_groups=mesh['cube'=8,'front'=64] {'front'}, dimensions={0}, use_global_device_ids=true | all-gather | bytes 266240 | tf_op jit(solution)/shard_map/all_gather | solution.py:45
  424.6 11.7 %cholesky.206 = f32[128,128]{1,0:T(8,128)S(1)} custom-call(f32[128,128]{1,0:T(8,128)S(1)} %copy.122), custom_call_target="Cholesky" | custom-call | tf_op jit(solution)/shard_map/jit(cholesky)/cholesky | solution.py:37
  437.0 9.8 %custom-call.17 = f32[1,128,128]{1,2,0:T(8,128)S(1)} custom-call(f32[1,128,128]{2,1,0:T(8,128)S(1)} %get-tuple-element.115), custom_call_target="InvertDiagBlocksLowerTriangular" | custom-call | tf_op jit(solution)/shard_map/jit(cholesky)/cholesky | solution.py:37
  447.5 11.7 %cholesky.223 = f32[128,128]{1,0:T(8,128)S(1)} custom-call(f32[128,128]{1,0:T(8,128)S(1)} %copy.124), custom_call_target="Cholesky" | custom-call | tf_op jit(solution)/shard_map/jit(cholesky)/cholesky | solution.py:37
  462.0 4.3 while.10
  466.3 19.7 %custom-call.18 = f32[2,128,128]{1,2,0:T(8,128)S(1)} custom-call(f32[2,128,128]{2,1,0:T(8,128)S(1)} %get-tuple-element.61), custom_call_target="InvertDiagBlocksLowerTriangular" | custom-call | tf_op jit(solution)/shard_map/jit(_solve_triangular)/triangular_solve | solution.py:51
  486.9 69.7 %all_to_all.19 = bf16[64,60,256]{2,1,0:T(8,128)(2,1)S(1)} all-to-all(bf16[64,60,256]{2,1,0:T(8,128)(2,1)S(1)} %tile.7), channel_id=1, replica_groups=mesh['cube'=8,'front'=64] {'front'}, dimensions={0} | all-to-all | bytes 3932160 | tf_op jit(solution)/shard_map/all_to_all | solution.py:13
  556.6 2.4 negate_bitcast_fusion.1
  561.7 2.2 slice_add_fusion.1
  563.9 2.0 reshape.282
  566.0 1.9 copy.129
  567.8 2.8 reshape.283
  570.7 2.4 collective-permute-start.2
  573.7 14.5 %collective-permute-done.2 = f32[60,3840]{1,0:T(8,128)S(1)} collective-permute-done((f32[60,3840]{1,0:T(8,128)S(1)}, f32[60,3840]{1,0:T(8,128)S(1)}, u32[]{:S(2)}, u32[]{:S(2)}) %collective-permute-start.2) | collective-permute-done | bytes 921632 | tf_op jit(solution)/shard_map/ppermute | solution.py:19
  589.6 4.5 reshape.284
  594.1 2.9 convolution_bitcast_fusion.1
  597.0 2.4 fusion.2
  602.3 2.9 reshape.286
  605.2 2.9 convolution_bitcast_fusion
  608.2 2.6 fusion
  612.0 1.7 reshape.287
  615.4 83.2 %all-gather.2 = f32[64,4,256]{2,1,0:T(4,128)S(1)} all-gather(f32[1,4,256]{2,1,0:T(4,128)S(1)} %slice_bitcast_fusion.15), channel_id=1, replica_groups=mesh['cube'=8,'front'=64] {'front'}, dimensions={0}, use_global_device_ids=true | all-gather | bytes 266240 | tf_op jit(solution)/shard_map/all_gather | solution.py:45
  699.1 11.7 %cholesky.240 = f32[128,128]{1,0:T(8,128)S(1)} custom-call(f32[128,128]{1,0:T(8,128)S(1)} %cholesky.276), custom_call_target="Cholesky" | custom-call | tf_op jit(solution)/shard_map/jit(cholesky)/cholesky | solution.py:37
  711.4 9.8 %custom-call.19 = f32[1,128,128]{1,2,0:T(8,128)S(1)} custom-call(f32[1,128,128]{2,1,0:T(8,128)S(1)} %get-tuple-element.111), custom_call_target="InvertDiagBlocksLowerTriangular" | custom-call | tf_op jit(solution)/shard_map/jit(cholesky)/cholesky | solution.py:37
  721.8 11.7 %cholesky.257 = f32[128,128]{1,0:T(8,128)S(1)} custom-call(f32[128,128]{1,0:T(8,128)S(1)} %convolution_subtract_fusion), custom_call_target="Cholesky" | custom-call | tf_op jit(solution)/shard_map/jit(cholesky)/cholesky | solution.py:37
  736.3 4.3 while.11
  740.6 19.7 %custom-call.20 = f32[2,128,128]{1,2,0:T(8,128)S(1)} custom-call(f32[2,128,128]{2,1,0:T(8,128)S(1)} %get-tuple-element.62), custom_call_target="InvertDiagBlocksLowerTriangular" | custom-call | tf_op jit(solution)/shard_map/jit(_solve_triangular)/triangular_solve | solution.py:51
  762.6 5.7 all-to-all-start.2
  771.3 53.6 %all-to-all-done.2 = bf16[64,60,256]{2,1,0:T(8,128)(2,1)S(1)} async-done(((bf16[64,60,256]{2,1,0:T(8,128)(2,1)}), bf16[64,60,256]{2,1,0:T(8,128)(2,1)S(1)}, u32[]{:S(2)}, u32[]{:S(2)}) %all-to-all-start.2) | async-done | bytes 1966112 | tf_op jit(solution)/shard_map/all_to_all | solution.py:13
  824.9 2.4 negate_bitcast_fusion
  830.0 2.2 slice_add_fusion
  832.2 2.0 reshape.291
  834.3 1.9 copy.140
  836.1 3.5 reshape.292
  (148 shorter events, 60.5 us)
Async XLA Ops:
  0.6 5.8 copy-start.2
  2.0 4.5 collective-permute-start
  299.5 16.0 %collective-permute-start.1 = (f32[60,3840]{1,0:T(8,128)S(1)}, f32[60,3840]{1,0:T(8,128)S(1)}, u32[]{:S(2)}, u32[]{:S(2)}) collective-permute-start(f32[60,3840]{1,0:T(8,128)S(1)} %reshape.272), channel_id=1, source_target_pairs={{0,128},{64,192},{128,0},{192,64},{256,384},{320,448},{384,256},{4... | collective-permute-start | bytes 2764808 | tf_op jit(solution)/shard_map/ppermute | solution.py:19
  327.7 1.7 copy-start
  570.7 17.5 %collective-permute-start.2 = (f32[60,3840]{1,0:T(8,128)S(1)}, f32[60,3840]{1,0:T(8,128)S(1)}, u32[]{:S(2)}, u32[]{:S(2)}) collective-permute-start(f32[60,3840]{1,0:T(8,128)S(1)} %reshape.283), channel_id=1, source_target_pairs={{0,256},{64,320},{128,384},{192,448},{256,0},{320,64},{384,128},{4... | collective-permute-start | bytes 2764808 | tf_op jit(solution)/shard_map/ppermute | solution.py:19
  600.7 1.7 copy-start.1
  762.6 62.4 %all-to-all-start.2 = ((bf16[64,60,256]{2,1,0:T(8,128)(2,1)}), bf16[64,60,256]{2,1,0:T(8,128)(2,1)S(1)}, u32[]{:S(2)}, u32[]{:S(2)}) async-start(bf16[64,60,256]{2,1,0:T(8,128)(2,1)} %tile.8), calls=%async_computation.2 | async-start | bytes 4194304 | tf_op jit(solution)/shard_map/all_to_all | solution.py:13
